TPU v7x, 512 devices: a whole 4x8x8 slice. The times are simulated.
512 devices in a mesh: dp: 128 (over y, z, core), mp: 4 (over x).
Axes of the slice: x: 4, y: 8, z: 8, core: 2. Of those that a mesh axis runs over, the one named last changes fastest.
Arguments:
- train_down: bfloat16 [64, 1024, 7168], P(None, 'dp', 'mp')
- owner: int32 [64], replicated, may hold values from 0 to 63, each once
- trainer_slot: int32 [64], replicated, may hold values from 0 to 63, each once
- expert_act: bfloat16 [4096, 8, 1024], P(('dp', 'mp')), may hold values from -6 to 6
- picks: int32 [4096, 8], P(('dp', 'mp')), may hold values from 0 to 63, all different within a row; in each aligned block of 8 rows (0 to 7, 8 to 15, ...) at most 2 rows name the same one
- route_logits: float32 [4096, 8], P(('dp', 'mp')), may hold values from -6 to 6
- queries: bfloat16 [128, 128, 576], P('dp')
- kv_cache: bfloat16 [128, 2048, 576], P('dp', 'mp')
- lengths: int32 [128], P('dp'), may hold values from 2 to 2048, as said below
Outputs:
- rollout_down: bfloat16 [128, 1024, 3584], P('dp', None, 'mp')
- rollout_scale: float32 [128, 8, 28], P('dp', None, 'mp')
- moe_out: bfloat16 [4096, 7168], P(('dp', 'mp'))
- context: bfloat16 [128, 128, 512], P('dp')
Inputs may be any that keep to these rules, and one draw needn't show every extreme that they name: owner gives each expert its own group. trainer_slot gives each expert its own block. `picks`: each row names 8 different experts; within the rows of one device no expert is named more than 2 times, and in some device exactly 2 times. `lengths`: the first sequence has exactly 2048 live positions.
All inputs are finite; a program needn't handle non-finite values.
Results may differ from a plain program's by a relative error of at most 0.017.
Values may be sent and summed in bfloat16 or wider, within the bound.
A program may use at most 64 MiB of HBM per device.

v0:
```python
import jax
import jax.numpy as jnp
from jax import lax
from jax.sharding import PartitionSpec as P

LATENT = 512


SCORE_SCALE = 192.0 ** (-0.5)
ROUTE_SCALE = 2.5
CODE_TOP = 448.0
EPS = 1e-06


def per_device(
    train_down, owner, trainer_slot, expert_act, picks, route_logits, queries, kv_cache, lengths
):
    ndp = lax.axis_size("dp")
    nmp = lax.axis_size("mp")
    experts, rows_part, col_part = train_down.shape
    wide = col_part // 2
    hidden = rows_part * ndp
    holder = jnp.argsort(owner)
    dest_group = jnp.arange(ndp) // 2
    dest_half = jnp.arange(ndp) % 2
    source_block = trainer_slot[holder[dest_group]] * 2 + dest_half
    split_cols = (
        train_down.reshape(experts, rows_part, 2, wide)
        .transpose(0, 2, 1, 3)
        .reshape(experts * 2, rows_part, wide)
    )
    outgoing_weights = split_cols[source_block]
    incoming = lax.all_to_all(outgoing_weights, "dp", split_axis=0, concat_axis=0, tiled=True)
    blocks = incoming.reshape(hidden // 128, 128, wide // 128, 128).astype(jnp.float32)
    scales = (jnp.max(jnp.abs(blocks), axis=(1, 3)) + EPS) / CODE_TOP
    coded = (blocks / scales[:, None, :, None]).astype(jnp.bfloat16)
    usable = (
        (coded.astype(jnp.float32) * scales[:, None, :, None])
        .astype(jnp.bfloat16)
        .reshape(hidden, wide)
    )
    rollout_down = coded.reshape(1, hidden, wide)
    rollout_scale = scales.reshape(1, hidden // 128, wide // 128)
    local_rows, topk = picks.shape
    capacity = 2 * max(1, local_rows * topk // experts)
    npick = local_rows * topk
    flat_picks = picks.reshape(-1)
    hits = (flat_picks[:, None] == jnp.arange(experts)[None, :]).astype(jnp.int32)
    before = jnp.cumsum(hits, axis=0) - hits
    place = jnp.sum(before * hits, axis=1)
    slot = flat_picks * capacity + place
    chooser = (jnp.arange(experts * capacity)[:, None] == slot[None, :]).astype(jnp.bfloat16)
    packed = jnp.dot(
        chooser, expert_act.reshape(npick, hidden), preferred_element_type=jnp.float32
    ).astype(jnp.bfloat16)
    by_group = packed.reshape(experts, capacity, hidden)[holder]
    outgoing_rows = jnp.repeat(by_group, 2, axis=0)
    arrived = lax.all_to_all(outgoing_rows, "dp", split_axis=0, concat_axis=0, tiled=True)
    span = kv_cache.shape[1]
    offset = lax.axis_index("mp") * span
    scores = (
        jnp.einsum("nhc,njc->nhj", queries, kv_cache, preferred_element_type=jnp.float32)
        * SCORE_SCALE
    )
    live = ((offset + jnp.arange(span))[None, :] < lengths[:, None])[:, None, :]
    masked = jnp.where(live, scores, -1e30)
    peak = jnp.max(masked, axis=2)
    probs = jnp.where(live, jnp.exp(masked - peak[..., None]), 0.0)
    total = jnp.sum(probs, axis=2)
    mixed_ctx = jnp.einsum(
        "nhj,njc->nhc",
        probs.astype(jnp.bfloat16),
        kv_cache[:, :, :LATENT],
        preferred_element_type=jnp.float32,
    )
    top = lax.pmax(peak, "mp")
    factor = jnp.exp(peak - top)
    total, mixed_ctx = (
        lax.psum((total * factor).astype(jnp.bfloat16), "mp").astype(jnp.float32),
        lax.psum((mixed_ctx * factor[..., None]).astype(jnp.bfloat16), "mp").astype(jnp.float32),
    )
    context = (mixed_ctx / total[..., None]).astype(jnp.bfloat16)
    piece = lax.all_gather(arrived, "mp", axis=0, tiled=True)
    count = piece.shape[0]
    result = jnp.dot(piece.reshape(-1, hidden), usable, preferred_element_type=jnp.float32).astype(
        jnp.bfloat16
    )
    produced = result.reshape(count, capacity, wide)
    produced = produced.reshape(nmp, ndp, capacity, wide)
    step_one = lax.all_to_all(produced, "mp", split_axis=0, concat_axis=0, tiled=True)
    returned = lax.all_to_all(step_one, "dp", split_axis=1, concat_axis=1, tiled=True)
    full = (
        returned.reshape(nmp, experts, 2, capacity, wide)
        .transpose(1, 3, 0, 2, 4)
        .reshape(experts, capacity, nmp * 2 * wide)
    )
    per_expert = full[owner].reshape(experts * capacity, nmp * 2 * wide)
    gathered = per_expert[slot].reshape(local_rows, topk, nmp * 2 * wide)
    gates = jax.nn.sigmoid(route_logits)
    shares = gates / jnp.sum(gates, axis=1, keepdims=True)
    combined = jnp.einsum("rk,rkd->rd", shares, gathered.astype(jnp.float32))
    moe_out = (ROUTE_SCALE * combined).astype(jnp.bfloat16)
    return (rollout_down, rollout_scale, moe_out, context)


def solution(mesh):
    placed = (
        P(None, "dp", "mp"),
        P(),
        P(),
        P(("dp", "mp"), None, None),
        P(("dp", "mp"), None),
        P(("dp", "mp"), None),
        P("dp", None, None),
        P("dp", "mp", None),
        P("dp"),
    )
    return jax.shard_map(
        per_device,
        mesh=mesh,
        in_specs=placed,
        out_specs=(
            P("dp", None, "mp"),
            P("dp", None, "mp"),
            P(("dp", "mp"), None),
            P("dp", None, None),
        ),
        check_vma=False,
    )
```

profile of v0, /device:TPU:1, one launch (start us, length us, event | category | flops | bytes accessed | tf_op | source)
XLA Modules:
  0.0 267.6 jit_solution(13143210033836701296)
XLA Ops:
  8.4 1.1 convolution_convert_fusion
  9.6 2.7 %sort.17 = (s32[64]{0:T(128)}, s32[64]{0:T(128)S(1)}) sort(s32[64]{0:T(128)} %param.10, s32[64]{0:T(128)S(1)} %iota.25), dimensions={0}, to_apply=%region_0.0 | sort | flops 384 | bytes 1024 | tf_op jit(solution)/shard_map/jit(argsort)/sort | solution.py:23
  12.3 1.1 gather_fusion.3
  14.5 18.4 %all-to-all-start.1 = ((bf16[128,2,1024]{2,1,0:T(2,128)(2,1)}), bf16[128,2,1024]{2,1,0:T(2,128)(2,1)S(1)}, u32[]{:S(2)}, u32[]{:S(2)}) async-start(bf16[128,2,1024]{2,1,0:T(2,128)(2,1)} %bitcast.11), calls=%async_computation.1 | async-start | bytes 1048576 | tf_op jit(solution)/shard_map/all_to_all | solution.py:58
  32.9 1.2 gather_fusion
  34.2 1.2 gather_fusion.1
  35.5 1.6 fusion.36
  37.2 2.0 gather_fusion.2
  39.2 13.2 %all-to-all-done.1 = bf16[128,2,1024]{2,1,0:T(2,128)(2,1)S(1)} async-done(((bf16[128,2,1024]{2,1,0:T(2,128)(2,1)}), bf16[128,2,1024]{2,1,0:T(2,128)(2,1)S(1)}, u32[]{:S(2)}, u32[]{:S(2)}) %all-to-all-start.1) | async-done | bytes 524320 | tf_op jit(solution)/shard_map/all_to_all | solution.py:58
  53.2 7.3 %all-to-all-start = ((bf16[128,8,896]{2,1,0:T(8,128)(2,1)}), bf16[128,8,896]{2,1,0:T(8,128)(2,1)S(1)}, u32[]{:S(2)}, u32[]{:S(2)}) async-start(bf16[128,8,896]{2,1,0:T(8,128)(2,1)} %gather_fusion.2), calls=%async_computation | async-start | bytes 3670016 | tf_op jit(solution)/shard_map/all_to_all | solution.py:33
  61.2 45.8 %all-to-all-done = bf16[128,8,896]{2,1,0:T(8,128)(2,1)S(1)} async-done(((bf16[128,8,896]{2,1,0:T(8,128)(2,1)}), bf16[128,8,896]{2,1,0:T(8,128)(2,1)S(1)}, u32[]{:S(2)}, u32[]{:S(2)}) %all-to-all-start) | async-done | bytes 1835040 | tf_op jit(solution)/shard_map/all_to_all | solution.py:33
  107.0 1.2 abs_reduce_fusion
  108.4 3.2 %reshape.302 = f32[8,128,7,128]{3,2,1,0:T(8,128)} reshape(bf16[128,8,896]{2,1,0:T(8,128)(2,1)S(1)} %all-to-all-done) | data formatting | bytes 5505024 | tf_op jit(solution)/shard_map/convert_element_type | solution.py:34
  111.6 4.1 %multiply_convert_fusion = bf16[8,128,7,128]{3,2,1,0:T(8,128)(2,1)} fusion(f32[8,7]{1,0:T(8,128)S(1)} %get-tuple-element.29, f32[8,128,7,128]{3,2,1,0:T(8,128)} %reshape.302), kind=kLoop, calls=%fused_computation.6 | loop fusion | flops 4587520 | bytes 5505248 | tf_op jit(solution)/shard_map/convert_element_type | solution.py:39
  115.7 4.1 %reshape.293 = bf16[1024,1024]{1,0:T(8,128)(2,1)} reshape(bf16[512,2,1024]{2,1,0:T(2,128)(2,1)} %all-gather.2.cloned.1.call-done) | data formatting | bytes 4194304 | tf_op jit(solution)/shard_map/reshape | solution.py:85
  119.8 5.8 %fusion.4 = bf16[1024,896]{1,0:T(8,128)(2,1)} fusion(bf16[1024,1024]{1,0:T(8,128)(2,1)} %reshape.293, bf16[128,8,7,128]{3,2,1,0:T(8,128)(2,1)} %bitcast.83), kind=kOutput, calls=%fused_computation.15 | convolution fusion | flops 1879965696 | bytes 5767168 | tf_op jit(solution)/shard_map/dot_general | solution.py:85
  125.6 4.8 %reshape_reshape.3 = bf16[4,128,2,896]{3,2,1,0:T(2,128)(2,1)} reshape(bf16[1024,896]{1,0:T(8,128)(2,1)} %fusion.4) | data formatting | bytes 3670016 | tf_op jit(solution)/shard_map/reshape;reshape | solution.py:89
  130.4 25.9 %all_to_all.20 = bf16[4,128,2,896]{3,2,1,0:T(2,128)(2,1)S(1)} all-to-all(bf16[4,128,2,896]{3,2,1,0:T(2,128)(2,1)} %reshape_reshape.3), channel_id=1, replica_groups=mesh['dp'=128,'mp'=4] {'mp'}, dimensions={0} | all-to-all | bytes 3670016 | tf_op jit(solution)/shard_map/all_to_all | solution.py:90
  156.3 2.5 copy.37
  158.8 10.4 %all-to-all-start.3 = ((bf16[4,128,2,896]{3,2,0,1:T(2,128)(2,1)}), bf16[4,128,2,896]{3,2,0,1:T(2,128)(2,1)}, u32[]{:S(2)}, u32[]{:S(2)}) async-start(bf16[4,128,2,896]{3,2,0,1:T(2,128)(2,1)} %copy.37), calls=%async_computation.3 | async-start | bytes 3670016 | tf_op jit(solution)/shard_map/all_to_all | solution.py:91
  170.3 7.7 %pmax.7 = f32[1,128]{1,0:T(1,128)S(1)} all-reduce(f32[1,128]{1,0:T(1,128)S(1)} %bitcast.85), channel_id=1, replica_groups=mesh['dp'=128,'mp'=4] {'mp'}, use_global_device_ids=true, to_apply=%region_7.8 | all-reduce | flops 128 | bytes 1024 | tf_op jit(solution)/shard_map/pmax | solution.py:76
  179.6 7.6 %psum.15 = bf16[128]{0:T(256)(128)(2,1)S(1)} all-reduce(bf16[128]{0:T(256)(128)(2,1)S(1)} %get-tuple-element.30), channel_id=1, replica_groups=mesh['dp'=128,'mp'=4] {'mp'}, use_global_device_ids=true, to_apply=%region_10.11 | all-reduce | flops 128 | bytes 512 | tf_op jit(solution)/shard_map/psum | solution.py:79
  187.2 41.9 %all-reduce.2.cloned.1.call-done = bf16[1,128,512]{2,1,0:T(8,128)(2,1)} async-done(((bf16[1,128,512]{2,1,0:T(8,128)(2,1)}), bf16[1,128,512]{2,1,0:T(8,128)(2,1)}) %all-reduce.2.cloned.1.call-update) | async-done | bytes 131088 | tf_op jit(solution)/shard_map/psum | solution.py:80
  229.1 1.7 divide_convert_fusion.1
  230.7 2.3 div.67
  233.0 4.9 %reshape.355 = f32[1,1024,896]{2,1,0:T(8,128)} reshape(f32[8,128,7,128]{3,2,1,0:T(8,128)} %div.67) | data formatting | bytes 7340032 | tf_op jit(solution)/shard_map/div | solution.py:36
  238.5 4.0 %fusion = bf16[1,1024,896]{2,1,0:T(8,128)(2,1)} fusion(f32[1,1024,896]{2,1,0:T(8,128)} %reshape.355, bf16[128,8,896]{2,1,0:T(8,128)(2,1)S(1)} %all-to-all-done), kind=kLoop, calls=%fused_computation.9 | loop fusion | flops 2752512 | bytes 7340032 | tf_op jit(solution)/shard_map/convert_element_type | solution.py:36
  242.5 2.9 %copy.47 = bf16[64,2,4,2,896]{4,3,2,1,0:T(2,128)(2,1)S(1)} copy(bf16[64,2,4,2,896]{4,1,2,3,0:T(2,128)(2,1)} %bitcast.14) | data formatting | bytes 3670016 | tf_op jit(solution)/shard_map/reshape | solution.py:95
  245.5 2.2 reshape.357
  247.7 6.9 %gather_fusion.4 = bf16[64,2,7168]{2,1,0:T(2,128)(2,1)} fusion(bf16[64,2,7168]{2,1,0:T(2,128)(2,1)} %reshape.357, s32[1024]{0:T(1024)S(1)} %pad_clamp_fusion.1), kind=kCustom, calls=%fused_computation.4 | custom fusion | bytes 3670272 | tf_op jit(solution)/shard_map/gather | solution.py:97
  254.5 4.1 %reshape.296 = bf16[128,7168]{1,0:T(8,128)(2,1)S(1)} reshape(bf16[64,2,7168]{2,1,0:T(2,128)(2,1)} %gather_fusion.4) | data formatting | bytes 3670016 | tf_op jit(solution)/shard_map/reshape | solution.py:97
  258.6 1.1 gather_fusion.5
  (57 shorter events, 8.0 us)
Async XLA Ops:
  7.2 162.8 %copy-start = (bf16[1,128,576]{1,2,0:T(8,128)(2,1)S(1)}, bf16[1,128,576]{1,2,0:T(8,128)(2,1)}, u32[]{:S(2)}) copy-start(bf16[1,128,576]{1,2,0:T(8,128)(2,1)} %param.15) | copy-start | bytes 442372
  8.4 25.8 %copy-start.1 = (s32[64]{0:T(128)S(1)}, s32[64]{0:T(128)}, u32[]{:S(2)}) copy-start(s32[64]{0:T(128)} %param.11) | copy-start | bytes 772
  14.5 37.9 %all-to-all-start.1 = ((bf16[128,2,1024]{2,1,0:T(2,128)(2,1)}), bf16[128,2,1024]{2,1,0:T(2,128)(2,1)S(1)}, u32[]{:S(2)}, u32[]{:S(2)}) async-start(bf16[128,2,1024]{2,1,0:T(2,128)(2,1)} %bitcast.11), calls=%async_computation.1 | async-start | bytes 1048576 | tf_op jit(solution)/shard_map/all_to_all | solution.py:58
  52.4 0.8 copy-start.2
  53.2 53.8 %all-to-all-start = ((bf16[128,8,896]{2,1,0:T(8,128)(2,1)}), bf16[128,8,896]{2,1,0:T(8,128)(2,1)S(1)}, u32[]{:S(2)}, u32[]{:S(2)}) async-start(bf16[128,8,896]{2,1,0:T(8,128)(2,1)} %gather_fusion.2), calls=%async_computation | async-start | bytes 3670016 | tf_op jit(solution)/shard_map/all_to_all | solution.py:33
  60.5 55.2 %all-gather.2.cloned.1.call-start = ((), (), s32[]{:S(2)}) async-start(), calls=%async_computation.4 | async-start | bytes 2621440 | tf_op jit(solution)/shard_map/all_gather | solution.py:83
  158.8 11.2 %copy-start.3 = (bf16[1,512,576]{1,2,0:T(8,128)(2,1)S(1)}, bf16[1,512,576]{1,2,0:T(8,128)(2,1)}, u32[]{:S(2)}) copy-start(bf16[1,512,576]{1,2,0:T(8,128)(2,1)} %param.16) | copy-start | bytes 1769476
  158.8 83.8 %all-to-all-start.3 = ((bf16[4,128,2,896]{3,2,0,1:T(2,128)(2,1)}), bf16[4,128,2,896]{3,2,0,1:T(2,128)(2,1)}, u32[]{:S(2)}, u32[]{:S(2)}) async-start(bf16[4,128,2,896]{3,2,0,1:T(2,128)(2,1)} %copy.37), calls=%async_computation.3 | async-start | bytes 3670016 | tf_op jit(solution)/shard_map/all_to_all | solution.py:91
  169.2 10.0 %copy-start.4 = (s32[8,8]{1,0:T(8,128)S(1)}, s32[8,8]{1,0:T(8,128)}, u32[]{:S(2)}) copy-start(s32[8,8]{1,0:T(8,128)} %param.13) | copy-start | bytes 772
  169.2 10.1 %copy-start.5 = (f32[8,8]{1,0:T(8,128)S(1)}, f32[8,8]{1,0:T(8,128)}, u32[]{:S(2)}) copy-start(f32[8,8]{1,0:T(8,128)} %param.14) | copy-start | bytes 772
  169.2 10.2 %copy-start.6 = (s32[64]{0:T(128)S(1)}, s32[64]{0:T(128)}, u32[]{:S(2)}) copy-start(s32[64]{0:T(128)} %param.10) | copy-start | bytes 772
  169.2 59.8 %all-reduce.2.cloned.1.call-start = ((), (), s32[]{:S(2)}) async-start(), calls=%async_computation.5 | async-start | bytes 262144 | tf_op jit(solution)/shard_map/psum | solution.py:80
Sparse Core Ops, SparseCore 0:
  63.4 37.0 all-gather.1
  179.3 49.6 all-reduce.1
where the time goes:
time: 270 us; the launch traced here: 268 us
  waiting for transfers between devices  101 us (37%)
  local copies, waits for them, and re-layouts  49.7 us (18%)
  blocking collectives  41.1 us (15%)
  starting transfers between devices  36.4 us (13%)
  other arithmetic  15.4 us (6%)
  between operations  15 us (6%)
  matrix products  8.64 us (3%)
    all_to_all x1, waiting for transfers between devices, per_device(): lax.all_to_all(outgoing_weights, 'dp', split_axis=0, concat_axis=0, tiled...  45.8 us
    psum x1, waiting for transfers between devices, per_device(): lax.psum((mixed_ctx * factor[..., None]).astype(jnp.bfloat16), 'mp')  41.9 us
    all_to_all x1, blocking collectives, per_device(): lax.all_to_all(produced, 'mp', split_axis=0, concat_axis=0, tiled=True)  25.9 us
    all_to_all x1, starting transfers between devices, per_device(): lax.all_to_all(outgoing_rows, 'dp', split_axis=0, concat_axis=0, tiled=True)  18.4 us
    all_to_all x1, waiting for transfers between devices, per_device(): lax.all_to_all(outgoing_rows, 'dp', split_axis=0, concat_axis=0, tiled=True)  13.2 us
    all_to_all x1, starting transfers between devices, per_device(): lax.all_to_all(step_one, 'dp', split_axis=1, concat_axis=1, tiled=True)  10.4 us
    pmax x1, blocking collectives, per_device(): top = lax.pmax(peak, 'mp')  7.68 us
    psum x1, blocking collectives, per_device(): lax.psum((total * factor).astype(jnp.bfloat16), 'mp').astype(jnp.float32)  7.59 us
  transfers between devices with their start and end apart: 5, of which 3 were waited for; matrix products, arithmetic and copies ran while one was open for 11% of the time, Pallas kernels for 0%

commit v1 on v0

v1 whole, which is shorter than its diff:
```python
import jax
import jax.numpy as jnp
from jax import lax
from jax.experimental import pallas as pl
from jax.experimental.pallas import tpu as pltpu
from jax.sharding import PartitionSpec as P

LATENT = 512
SCORE_SCALE = 192.0 ** (-0.5)
ROUTE_SCALE = 2.5
CODE_TOP = 448.0
EPS = 1e-06

MESH = pl.DeviceIdType.MESH
F32 = jnp.float32
BF16 = jnp.bfloat16
RING = 8
WIDE = 896
HIDDEN = 1024
BLOCKS = WIDE // 128


def mod8(v):
    return lax.rem(v + 8 * RING, RING)


def kernel(
    src_ref,
    len_ref,
    row_ref,
    coef_ref,
    td_ref,
    act_ref,
    q_ref,
    kv_ref,
    down_ref,
    scale_ref,
    moe_ref,
    ctx_ref,
    wsend,
    wrecv,
    asend,
    arecv,
    bsend,
    afull,
    usable,
    psend,
    precv,
    cbuf,
    xacc,
    xstat,
    moesend,
    moerecv,
    macc,
    scl,
    a_send,
    a_recv,
    b_send,
    b_recv,
    c_send,
    c_recv,
    k_send,
    k_recv,
    w_send,
    w_recv,
    p_send,
    p_recv,
    x_send,
    x_recv,
    m_send,
    m_recv,
):
    d = lax.axis_index("dp")
    m = lax.axis_index("mp")
    line = lax.div(d, 2)
    c = lax.rem(d, 2)
    y = lax.div(line, RING)
    z = lax.rem(line, RING)
    j = c * 4 + m

    def remote(src, dst, send, recv, dt, mt):
        return pltpu.make_async_remote_copy(
            src_ref=src,
            dst_ref=dst,
            send_sem=send,
            recv_sem=recv,
            device_id=(dt, mt),
            device_id_type=MESH,
        )

    def drain(ref, sem):
        pltpu.make_async_copy(ref, ref, sem).wait()

    def mate(k):
        return 2 * line + lax.div(k, 4), lax.rem(k, 4)

    barrier = pltpu.get_barrier_semaphore()

    def greet(i, _):
        pl.semaphore_signal(
            barrier, inc=1, device_id=(lax.rem(d + i, 128), m), device_id_type=MESH
        )
        return 0

    lax.fori_loop(1, 128, greet, 0)
    for dx in range(1, 4):
        for cc in range(2):
            pl.semaphore_signal(
                barrier,
                inc=1,
                device_id=(2 * line + cc, lax.rem(m + dx, 4)),
                device_id_type=MESH,
            )

    acts = act_ref[...].astype(F32).reshape(64, HIDDEN).astype(BF16)
    chooser = (
        (lax.broadcasted_iota(jnp.int32, (128, 64), 0) == row_ref[...]).astype(F32).astype(BF16)
    )
    packed = jnp.dot(chooser, acts, preferred_element_type=F32).astype(BF16)
    asend[...] = packed.reshape(RING, 16, HIDDEN)
    arecv[j] = asend[j]
    cbuf[m] = coef_ref[...]

    pl.semaphore_wait(barrier, 133)

    def a_copy(dj):
        jt = lax.rem(j + dj, RING)
        dt, mt = mate(jt)
        return remote(asend.at[jt], arecv.at[j], a_send.at[dj], a_recv.at[j], dt, mt)

    def a_arrival(dj):
        js = lax.rem(j + dj, RING)
        return remote(asend.at[js], arecv.at[js], a_send.at[dj], a_recv.at[js], d, m)

    for dj in range(1, RING):
        a_copy(dj).start()

    def k_copy(dx):
        mt = lax.rem(m + dx, 4)
        return remote(coef_ref, cbuf.at[m], k_send.at[dx], k_recv.at[m], d, mt)

    for dx in range(1, 4):
        k_copy(dx).start()

    def w_line(t):
        a = lax.div(t, 32)
        b = lax.rem(t, 32)
        b4 = lax.rem(b, 4)
        dy = 2 * b4 + a
        dz = lax.rem(lax.div(b, 4) + 2 * b4, RING)
        return mod8(y + dy) * RING + mod8(z + dz)

    def w_step(t, _):
        lt = w_line(t)
        blk = td_ref[src_ref[lt]]
        for cc in range(2):
            wsend[2 * t + cc] = blk[:, cc * WIDE : (cc + 1) * WIDE]
        for cc in range(2):
            dt = 2 * lt + cc
            remote(wsend.at[2 * t + cc], wrecv.at[d], w_send, w_recv.at[y], dt, m).start()
        return 0

    own = td_ref[src_ref[line]]
    for cc in range(2):
        wsend[cc] = own[:, cc * WIDE : (cc + 1) * WIDE]
    remote(wsend.at[1 - c], wrecv.at[d], w_send, w_recv.at[y], 2 * line + 1 - c, m).start()
    pltpu.make_async_copy(wsend.at[c], wrecv.at[d], w_recv.at[y]).start()
    lax.fori_loop(1, 8, w_step, 0)

    for dj in range(1, RING):
        a_arrival(dj).wait_recv()
    ro = lax.broadcasted_iota(jnp.int32, (128, 128), 0)
    co = lax.broadcasted_iota(jnp.int32, (128, 128), 1)
    want = lax.bitwise_and(lax.shift_right_logical(ro, 1), 7) * 16
    want = want + lax.shift_right_logical(ro, 4) * 2 + lax.bitwise_and(ro, 1)
    perm = (co == want).astype(F32).astype(BF16)
    regrouped = jnp.dot(perm, arecv[...].reshape(128, HIDDEN), preferred_element_type=F32)
    bsend[...] = regrouped.astype(BF16).reshape(RING, 16, HIDDEN)
    r_out = lax.rem(y + z, RING)
    r_in = mod8(j - y - z)

    def b_target(dy):
        yg = mod8(y + dy)
        return yg, yg * RING + mod8(j - y - z - yg)

    def b_copy(dy):
        yg, gl = b_target(dy)
        return remote(
            bsend.at[yg], afull.at[r_out * RING + y], b_send.at[yg], b_recv, 2 * gl + c, m
        )

    for dy in range(RING):
        yg, gl = b_target(dy)

        @pl.when(gl != line)
        def _():
            b_copy(dy).start()

        @pl.when(gl == line)
        def _():
            pltpu.make_async_copy(bsend.at[yg], afull.at[r_out * RING + y], b_recv).start()

    lax.fori_loop(8, 32, w_step, 0)

    mine = afull.at[pl.ds(r_in * RING, RING)]
    drain(mine, b_recv)

    def c_copy(dj):
        dt, mt = mate(lax.rem(j + dj, RING))
        return remote(mine, mine, c_send.at[dj], c_recv.at[r_in], dt, mt)

    for dj in range(1, RING):
        c_copy(dj).start()

    lax.fori_loop(32, 64, w_step, 0)

    query = q_ref[0]
    cache = kv_ref[0]
    scores = (
        lax.dot_general(query, cache, (((1,), (1,)), ((), ())), preferred_element_type=F32)
        * SCORE_SCALE
    )
    span = scores.shape[1]
    live = (m * span + lax.broadcasted_iota(jnp.int32, scores.shape, 1)) < len_ref[0]
    masked = jnp.where(live, scores, -1e30)
    peak = jnp.max(masked, axis=1, keepdims=True)
    probs = jnp.where(live, jnp.exp(masked - peak), 0.0)
    total = jnp.sum(probs, axis=1, keepdims=True)
    mixed = jnp.dot(probs.astype(BF16), cache[:, :LATENT], preferred_element_type=F32)
    lane = lax.broadcasted_iota(jnp.int32, (128, 128), 1)
    xacc[m] = mixed.astype(BF16)
    xstat[m] = jnp.where(lane < 64, peak, total)

    def x_copies(dx):
        mt = lax.rem(m + dx, 4)
        return (
            remote(xacc.at[m], xacc.at[m], x_send.at[0, dx], x_recv.at[0, m], d, mt),
            remote(xstat.at[m], xstat.at[m], x_send.at[1, dx], x_recv.at[1, m], d, mt),
        )

    for dx in range(1, 4):
        for copy in x_copies(dx):
            copy.start()

    def quantize(i, _):
        dy = 2 * lax.rem(i, 4) + lax.div(i, 4)
        ys = mod8(y - dy)
        rows = wrecv.at[pl.ds(16 * ys, 16)]
        drain(rows, w_recv.at[ys])
        w = rows[...].astype(F32).reshape(128, WIDE)
        at = lax.broadcasted_iota(jnp.int32, (1, 128), 1)
        row = jnp.zeros((1, 128), F32)
        for b in range(BLOCKS):
            blk = w[:, b * 128 : (b + 1) * 128]
            top = jnp.max(jnp.max(jnp.abs(blk), axis=0, keepdims=True), axis=1, keepdims=True) + EPS
            scale = top / CODE_TOP
            coded = (blk * (CODE_TOP / top)).astype(BF16)
            down_ref[pl.ds(128 * ys, 128), b * 128 : (b + 1) * 128] = coded
            usable[pl.ds(128 * ys, 128), b * 128 : (b + 1) * 128] = (
                coded.astype(F32) * scale
            ).astype(BF16)
            row = jnp.where(at == b, scale, row)
        scl[pl.ds(ys, 1), :] = row
        return 0

    lax.fori_loop(0, 4, quantize, 0)

    for dx in range(1, 4):
        ms = lax.rem(m + dx, 4)
        remote(xacc.at[ms], xacc.at[ms], x_send.at[0, dx], x_recv.at[0, ms], d, m).wait_recv()
        remote(xstat.at[ms], xstat.at[ms], x_send.at[1, dx], x_recv.at[1, ms], d, m).wait_recv()
    peaks = [xstat[s][:, 0:1] for s in range(4)]
    highest = jnp.maximum(jnp.maximum(peaks[0], peaks[1]), jnp.maximum(peaks[2], peaks[3]))
    weight = jnp.zeros((128, 1), F32)
    blend = jnp.zeros((128, LATENT), F32)
    for s in range(4):
        factor = jnp.exp(peaks[s] - highest)
        weight = weight + xstat[s][:, 64:65] * factor
        blend = blend + xacc[s].astype(F32) * factor
    ctx_ref[...] = (blend / weight).astype(BF16)

    lax.fori_loop(4, 8, quantize, 0)
    scale_ref[...] = scl[:, 0:BLOCKS]

    for dj in range(1, RING):
        js = lax.rem(j + dj, RING)
        r = mod8(js - y - z)
        part = afull.at[pl.ds(r * RING, RING)]
        remote(part, part, c_send.at[dj], c_recv.at[r], d, m).wait_recv()

    def project(i, _):
        r = lax.rem(y + z + i, RING)
        rows = afull[pl.ds(r * RING, RING)].reshape(128, HIDDEN)
        out = jnp.dot(rows, usable[...], preferred_element_type=F32)
        psend[pl.ds(16 * i, 16)] = out.reshape(16, 8, WIDE).astype(BF16)

        def give(b, _):
            yt = mod8(y + lax.div(b, 2))
            cc = lax.rem(b, 2)
            dt = 2 * (yt * RING + mod8(r - yt)) + cc
            src = psend.at[16 * i + 2 * yt + cc]
            dst = precv.at[(r_out * 2 + c) * RING + y]

            @pl.when(dt != d)
            def _():
                remote(src, dst, p_send, p_recv.at[r_out], dt, m).start()

            @pl.when(dt == d)
            def _():
                pltpu.make_async_copy(src, dst, p_recv.at[r_out]).start()

            return 0

        lax.fori_loop(0, 16, give, 0)
        return 0

    lax.fori_loop(0, RING, project, 0)

    for dx in range(1, 4):
        ms = lax.rem(m + dx, 4)
        remote(coef_ref, cbuf.at[ms], k_send.at[dx], k_recv.at[ms], d, m).wait_recv()
    macc[...] = jnp.zeros_like(macc)

    def combine(i, _):
        r = mod8(y + z - i)
        drain(precv.at[pl.ds(16 * r, 16)], p_recv.at[r])
        share = jnp.concatenate([cbuf[s, r] for s in range(4)], axis=0)[:, 0:64]
        high = share.astype(BF16)
        low = (share - high.astype(F32)).astype(BF16)
        both = jnp.concatenate([high, low], axis=0)
        for s in range(2):
            got = precv[pl.ds((2 * r + s) * RING, RING)].astype(F32).reshape(64, WIDE).astype(BF16)
            part = jnp.dot(both, got, preferred_element_type=F32)
            macc[s] += part[0:32] + part[32:64]
        return 0

    lax.fori_loop(0, RING, combine, 0)
    for s in range(4):
        for half in range(2):
            moesend[s, :, half * WIDE : (half + 1) * WIDE] = macc[half, 8 * s : 8 * s + 8].astype(
                BF16
            )

    def m_copy(dx):
        mt = lax.rem(m + dx, 4)
        return remote(moesend.at[mt], moerecv.at[m], m_send.at[dx], m_recv.at[m], d, mt)

    for dx in range(1, 4):
        m_copy(dx).start()
    moerecv[m] = moesend[m]
    for dx in range(1, 4):
        ms = lax.rem(m + dx, 4)
        remote(moesend.at[ms], moerecv.at[ms], m_send.at[dx], m_recv.at[ms], d, m).wait_recv()
    for s in range(4):
        moe_ref[:, s * 2 * WIDE : (s + 1) * 2 * WIDE] = moerecv[s]

    for dj in range(1, RING):
        a_copy(dj).wait_send()
        c_copy(dj).wait_send()
    for dx in range(1, 4):
        k_copy(dx).wait_send()
        m_copy(dx).wait_send()
        for copy in x_copies(dx):
            copy.wait_send()
    for dy in range(RING):
        yg, gl = b_target(dy)

        @pl.when(gl != line)
        def _():
            b_copy(dy).wait_send()

    drain(wsend.at[pl.ds(0, 127)], w_send)
    drain(psend.at[pl.ds(0, 127)], p_send)


def per_device(
    train_down, owner, trainer_slot, expert_act, picks, route_logits, queries, kv_cache, lengths
):
    d = lax.axis_index("dp")
    m = lax.axis_index("mp")
    line = d // 2
    y, z = line // RING, line % RING
    groups = jnp.arange(64, dtype=jnp.int32)
    source = jnp.sum(jnp.where(owner[None, :] == groups[:, None], trainer_slot[None, :], 0), axis=1)
    flat = picks.reshape(64)
    group = jnp.sum(jnp.where(flat[:, None] == groups[None, :], owner[None, :], 0), axis=1)
    earlier = (flat[:, None] == flat[None, :]) & (groups[None, :] < groups[:, None])
    place = jnp.sum(earlier.astype(jnp.int32), axis=1)
    diag = (group // RING + group % RING) % RING
    row = ((diag + y + z) % RING) * 16 + (group // RING) * 2 + place
    column = (group // RING) * 8 + m * 2 + place
    gates = jax.nn.sigmoid(route_logits)
    shares = ROUTE_SCALE * (gates / jnp.sum(gates, axis=1, keepdims=True))
    key = (diag * 128 + column).reshape(8, 8)
    spots = jnp.arange(RING * 128, dtype=jnp.int32).reshape(RING, 1, 1, 128)
    coef = jnp.sum(
        jnp.where(key[None, :, :, None] == spots, shares[None, :, :, None], 0.0), axis=2
    )

    vmem = pl.BlockSpec(memory_space=pltpu.VMEM)
    smem = pl.BlockSpec(memory_space=pltpu.SMEM)
    dma = pltpu.SemaphoreType.DMA
    down, scale, moe, context = pl.pallas_call(
        kernel,
        out_shape=(
            jax.ShapeDtypeStruct((HIDDEN, WIDE), BF16),
            jax.ShapeDtypeStruct((RING, BLOCKS), F32),
            jax.ShapeDtypeStruct((8, 8 * WIDE), BF16),
            jax.ShapeDtypeStruct((128, LATENT), BF16),
        ),
        in_specs=[smem, smem] + [vmem] * 6,
        out_specs=(vmem,) * 4,
        scratch_shapes=[
            pltpu.VMEM((128, 8, WIDE), BF16),
            pltpu.VMEM((128, 8, WIDE), BF16),
            pltpu.VMEM((RING, 16, HIDDEN), BF16),
            pltpu.VMEM((RING, 16, HIDDEN), BF16),
            pltpu.VMEM((RING, 16, HIDDEN), BF16),
            pltpu.VMEM((64, 16, HIDDEN), BF16),
            pltpu.VMEM((HIDDEN, WIDE), BF16),
            pltpu.VMEM((128, 8, WIDE), BF16),
            pltpu.VMEM((128, 8, WIDE), BF16),
            pltpu.VMEM((4, RING, 8, 128), F32),
            pltpu.VMEM((4, 128, LATENT), BF16),
            pltpu.VMEM((4, 128, 128), F32),
            pltpu.VMEM((4, 8, 2 * WIDE), BF16),
            pltpu.VMEM((4, 8, 2 * WIDE), BF16),
            pltpu.VMEM((2, 32, WIDE), F32),
            pltpu.VMEM((RING, 128), F32),
            dma((RING,)),
            dma((RING,)),
            dma((RING,)),
            dma,
            dma((RING,)),
            dma((RING,)),
            dma((4,)),
            dma((4,)),
            dma,
            dma((RING,)),
            dma,
            dma((RING,)),
            dma((2, 4)),
            dma((2, 4)),
            dma((4,)),
            dma((4,)),
        ],
        compiler_params=pltpu.CompilerParams(
            collective_id=0, has_side_effects=True, vmem_limit_bytes=48 * 1024 * 1024
        ),
        cost_estimate=pl.CostEstimate(
            flops=2_200_000_000, bytes_accessed=8_000_000, transcendentals=70_000
        ),
    )(source, lengths, row.reshape(1, 64), coef, train_down, expert_act, queries, kv_cache)
    return (
        down.reshape(1, HIDDEN, WIDE),
        scale.reshape(1, RING, BLOCKS),
        moe,
        context.reshape(1, 128, LATENT),
    )


def solution(mesh):
    placed = (
        P(None, "dp", "mp"),
        P(),
        P(),
        P(("dp", "mp"), None, None),
        P(("dp", "mp"), None),
        P(("dp", "mp"), None),
        P("dp", None, None),
        P("dp", "mp", None),
        P("dp"),
    )
    return jax.shard_map(
        per_device,
        mesh=mesh,
        in_specs=placed,
        out_specs=(
            P("dp", None, "mp"),
            P("dp", None, "mp"),
            P(("dp", "mp"), None),
            P("dp", None, None),
        ),
        check_vma=False,
    )
```

time: 270 us -> 144 us (0.53)
  Pallas kernels: 0 us -> 130 us
  waiting for transfers between devices: 101 us -> 0 us
  blocking collectives: 41.1 us -> 0 us
  local copies, waits for them, and re-layouts: 49.7 us -> 8.92 us
  starting transfers between devices: 36.4 us -> 0 us
  between operations: 15 us -> 1.37 us
  other arithmetic: 15.4 us -> 2.68 us
  matrix products: 8.64 us -> 0 us
    pallas_call x0 -> x1, Pallas kernels: none -> 130 us  [per_device(): pl.pallas_call(kernel, out_shape=(jax.ShapeDtypeStruct((HIDDEN, WIDE), BF...]
    all_to_all x3 -> x0, waiting for transfers between devices: 58.9 us -> none  [the longest x1 45.8 us: per_device(): lax.all_to_all(outgoing_weights, 'dp', split_axis=0, concat_axis=0, tiled...]
    psum x1 -> x0, waiting for transfers between devices: 41.9 us -> none  [per_device(): lax.psum((mixed_ctx * factor[..., None]).astype(jnp.bfloat16), 'mp')]
    all_to_all x3 -> x0, starting transfers between devices: 36.1 us -> none  [the longest x1 18.4 us: per_device(): lax.all_to_all(outgoing_rows, 'dp', split_axis=0, concat_axis=0, tiled=True)]
    all_to_all x1 -> x0, blocking collectives: 25.9 us -> none  [per_device(): lax.all_to_all(produced, 'mp', split_axis=0, concat_axis=0, tiled=True)]
    reshape x6 -> x0, local copies, waits for them, and re-layouts: 14.2 us -> none  [the longest x2 5.11 us: per_device(): full = returned.reshape(nmp, experts, 2, capacity, wide).transpose(1, 3,...]
    gather x6 -> x0, local copies, waits for them, and re-layouts: 13.5 us -> none  [the longest x1 6.85 us: per_device(): per_expert = full[owner].reshape(experts * capacity, nmp * 2 * wide)]
    convert_element_type x5 -> x0, other arithmetic: 10.6 us -> none  [the longest x1 4.09 us: per_device(): usable = (coded.astype(jnp.float32) * scales[:, None, :, None]).astype(jn...]
  transfers between devices with their start and end apart: 5 -> 0, of which waited for: 3 -> 0; matrix products, arithmetic and copies ran while one was open for 11% -> 0% of each run, Pallas kernels for 0% -> 0%
where the time goes in v1:
time: 144 us; the launch traced here: 143 us
  Pallas kernels  130 us (90%)
  local copies, waits for them, and re-layouts  8.92 us (6%)
  other arithmetic  2.68 us (2%)
    pallas_call x1, Pallas kernels, per_device(): pl.pallas_call(kernel, out_shape=(jax.ShapeDtypeStruct((HIDDEN, WIDE), BF...  130 us
    unnamed x10, local copies, waits for them, and re-layouts  8 us

profile of v1, /device:TPU:1, one launch (start us, length us, event | category | flops | bytes accessed | tf_op | source)
XLA Modules:
  0.0 143.1 jit_solution(8842336752424298557)
XLA Ops:
  1.3 0.8 eq.65
  2.1 0.8 divide_reduce_fusion
  2.9 0.9 select_reduce_fusion.1
  3.8 0.8 divide_multiply_fusion
  4.6 0.1 reduce_sum.58
  4.7 0.1 reduce_sum.59
  4.8 0.2 select_reduce_fusion.coef_ref
  4.9 1.1 copy.16.q_ref
  6.0 1.4 copy.17.kv_ref
  7.4 0.0 copy-start
  7.4 1.5 %copy-done = bf16[64,8,1792]{2,1,0:T(8,128)(2,1)S(1)} copy-done((bf16[64,8,1792]{2,1,0:T(8,128)(2,1)S(1)}, bf16[64,8,1792]{2,1,0:T(8,128)(2,1)}, u32[]{:S(2)}) %copy-start) | copy-done | bytes 1835032
  8.9 0.0 copy-start.1
  8.9 0.9 copy-done.1
  9.8 130.1 %shard_map.120 = (bf16[1024,896]{1,0:T(8,128)(2,1)S(1)}, f32[8,7]{1,0:T(8,128)S(1)}, bf16[8,7168]{1,0:T(8,128)(2,1)S(1)}, bf16[128,512]{1,0:T(8,128)(2,1)S(1)}) custom-call(s32[64]{0:T(128)S(1)} %get-tuple-element.22.src_ref, s32[1]{0:T(128)S(6)} %copy.22.len_ref, s32[1,64]{1,0:T(1,128)S(1)} %fusion.12.row_ref, f32[8,8,128]{2,1,0:T(8,128)S(1)} %select_reduce_fusion.coef_ref, ...), custom_call_target="tpu_custom_call" | custom-call | flops 2200000000 | bytes 8000000 | tf_op jit(solution)/shard_map/pallas_call | solution.py:403
  139.9 0.7 copy.18
  140.6 1.2 copy.23
  141.8 0.6 copy.24
  142.4 0.7 copy.25
  (3 shorter events, 0.1 us)
Async XLA Ops:
  7.4 1.5 %copy-start = (bf16[64,8,1792]{2,1,0:T(8,128)(2,1)S(1)}, bf16[64,8,1792]{2,1,0:T(8,128)(2,1)}, u32[]{:S(2)}) copy-start(bf16[64,8,1792]{2,1,0:T(8,128)(2,1)} %td_ref.1) | copy-start | bytes 5505028
  8.9 0.9 copy-start.1

commit v2 on v1

v2 whole, which is shorter than its diff:
```python
import jax
import jax.numpy as jnp
from jax import lax
from jax.experimental import pallas as pl
from jax.experimental.pallas import tpu as pltpu
from jax.sharding import PartitionSpec as P

LATENT = 512
SCORE_SCALE = 192.0 ** (-0.5)
ROUTE_SCALE = 2.5
CODE_TOP = 448.0
EPS = 1e-06

MESH = pl.DeviceIdType.MESH
F32 = jnp.float32
BF16 = jnp.bfloat16
RING = 8
WIDE = 896
HIDDEN = 1024
BLOCKS = WIDE // 128
LIMIT = 64 * 1024 * 1024
SIDE = (1, 7, 3, 5, 2, 6, 4, 0)


def mod8(v):
    return lax.rem(v + 8 * RING, RING)


def swing(h):
    half = lax.div(h + 1, 2)
    return mod8(jnp.where(lax.rem(h, 2) == 1, half, -half))


def offset(turn, b):
    return swing(lax.rem(turn + b, RING)), swing(b)


def kernel(
    src_ref,
    len_ref,
    owner_ref,
    picks_ref,
    logit_ref,
    td_hbm,
    act_hbm,
    q_hbm,
    kv_hbm,
    down_hbm,
    scale_hbm,
    moe_hbm,
    ctx_hbm,
    down_ref,
    scale_ref,
    moe_ref,
    ctx_ref,
    td_ref,
    act_ref,
    q_ref,
    kv_ref,
    coef_ref,
    wsend,
    wrecv,
    asend,
    arecv,
    bsend,
    afull,
    usable,
    psend,
    precv,
    qsend,
    qrecv,
    kline,
    kout,
    kfin,
    xacc,
    xstat,
    moesend,
    moerecv,
    scl,
    load,
    keep,
    a_send,
    a_recv,
    b_send,
    b_recv,
    c_send,
    c_recv,
    k_send,
    k_recv,
    l_send,
    l_recv,
    w_send,
    w_recv,
    p_send,
    p_recv,
    q_send,
    q_recv,
    x_send,
    x_recv,
    m_send,
    m_recv,
):
    d = lax.axis_index("dp")
    m = lax.axis_index("mp")
    line = lax.div(d, 2)
    c = lax.rem(d, 2)
    y = lax.div(line, RING)
    z = lax.rem(line, RING)
    j = c * 4 + m
    f = jnp.where(c == 0, z, y)
    g = jnp.where(c == 0, y, z)

    def at(ft, gt):
        return jnp.where(c == 0, gt, ft), jnp.where(c == 0, ft, gt)

    def fellow(ft, gt):
        yt, zt = at(ft, gt)
        return 2 * (yt * RING + zt) + c

    def remote(src, dst, send, recv, dt, mt):
        return pltpu.make_async_remote_copy(
            src_ref=src,
            dst_ref=dst,
            send_sem=send,
            recv_sem=recv,
            device_id=(dt, mt),
            device_id_type=MESH,
        )

    def drain(ref, sem):
        pltpu.make_async_copy(ref, ref, sem).wait()

    def mate(k):
        return 2 * line + lax.div(k, 4), lax.rem(k, 4)

    loads = [
        pltpu.make_async_copy(hbm, ref, load.at[n])
        for n, (hbm, ref) in enumerate(
            ((act_hbm, act_ref), (td_hbm, td_ref), (q_hbm, q_ref), (kv_hbm, kv_ref))
        )
    ]
    for copy in loads:
        copy.start()
    results = [
        pltpu.make_async_copy(ref, hbm, keep.at[n])
        for n, (hbm, ref) in enumerate(
            (
                (down_hbm, down_ref),
                (scale_hbm, scale_ref),
                (moe_hbm, moe_ref),
                (ctx_hbm, ctx_ref),
            )
        )
    ]

    barrier = pltpu.get_barrier_semaphore()

    def greet(i, _):
        pl.semaphore_signal(
            barrier, inc=1, device_id=(lax.rem(d + i, 128), m), device_id_type=MESH
        )
        return 0

    lax.fori_loop(1, 128, greet, 0)
    for dx in range(1, 4):
        for cc in range(2):
            pl.semaphore_signal(
                barrier,
                inc=1,
                device_id=(2 * line + cc, lax.rem(m + dx, 4)),
                device_id_type=MESH,
            )

    def iota(shape, axis):
        return lax.broadcasted_iota(jnp.int32, shape, axis)

    def low3(v):
        return lax.bitwise_and(v, 7)

    def high3(v):
        return lax.shift_right_logical(v, 3)

    def column_of(v):
        return jnp.sum(jnp.where(iota((64, 64), 0) == iota((64, 64), 1), v, 0), axis=1, keepdims=True)

    spread = (low3(iota((8, 64), 1)) == iota((8, 64), 0)).astype(F32).astype(BF16)
    held = high3(iota((8, 64), 1)) == iota((8, 64), 0)

    def along(v):
        return jnp.where(held, jnp.dot(v.astype(BF16), spread, preferred_element_type=F32), 0.0)

    flat = jnp.sum(along(picks_ref[...].astype(F32)), axis=0, keepdims=True).astype(jnp.int32)
    owner = column_of(owner_ref[...])
    group = jnp.sum(jnp.where(iota((64, 64), 0) == flat, owner, 0), axis=0, keepdims=True)
    twin = (column_of(flat) == flat) & (iota((64, 64), 0) < iota((64, 64), 1))
    place = jnp.sum(twin.astype(jnp.int32), axis=0, keepdims=True)
    yg, zg = high3(group), low3(group)
    gates = jax.nn.sigmoid(logit_ref[...])
    shares = ROUTE_SCALE * (gates / jnp.sum(gates, axis=1, keepdims=True))
    coarse = shares.astype(BF16).astype(F32)
    coarse, fine = along(coarse).astype(BF16), along(shares - coarse).astype(BF16)
    for core, (gt, ft) in enumerate(((yg, zg), (zg, yg))):
        key = column_of(gt * 128 + ft * 16 + j * 2 + place)
        spots = (iota((64, 1024), 1) == key).astype(F32).astype(BF16)
        coef = jnp.dot(coarse, spots, preferred_element_type=F32)
        coef += jnp.dot(fine, spots, preferred_element_type=F32)
        for n in range(RING):
            coef_ref[core, n] = coef[:, n * 128 : (n + 1) * 128]
    kline[j] = coef_ref[c]

    row = low3(yg + zg + y + z) * 16 + yg * 2 + place
    chooser = (iota((128, 64), 0) == row).astype(F32).astype(BF16)
    loads[0].wait()
    acts = act_ref[...].astype(F32).reshape(64, HIDDEN).astype(BF16)
    packed = jnp.dot(chooser, acts, preferred_element_type=F32).astype(BF16)
    asend[...] = packed.reshape(RING, 16, HIDDEN)
    arecv[j] = asend[j]

    pl.semaphore_wait(barrier, 133)

    def a_copy(dj):
        jt = lax.rem(j + dj, RING)
        dt, mt = mate(jt)
        return remote(asend.at[jt], arecv.at[j], a_send.at[dj], a_recv.at[j], dt, mt)

    def a_arrival(dj):
        js = lax.rem(j + dj, RING)
        return remote(asend.at[js], arecv.at[js], a_send.at[dj], a_recv.at[js], d, m)

    for dj in range(1, RING):
        a_copy(dj).start()

    def k_copy(dj):
        jt = lax.rem(j + dj, RING)
        dt, mt = mate(jt)
        src = coef_ref.at[lax.div(jt, 4)]
        return remote(src, kline.at[j], k_send.at[dj], k_recv.at[j], dt, mt)

    for dj in range(1, RING):
        k_copy(dj).start()

    def w_line(t):
        dy, dz = offset(lax.div(t, RING), lax.rem(t, RING))
        return mod8(y + dy) * RING + mod8(z + dz)

    def w_step(t, _):
        lt = w_line(t)
        blk = td_ref[src_ref[lt]]
        for cc in range(2):
            wsend[2 * t + cc] = blk[:, cc * WIDE : (cc + 1) * WIDE]
        for cc in range(2):
            dt = 2 * lt + cc
            remote(wsend.at[2 * t + cc], wrecv.at[d], w_send, w_recv.at[y], dt, m).start()
        return 0

    loads[1].wait()
    own = td_ref[src_ref[line]]
    for cc in range(2):
        wsend[cc] = own[:, cc * WIDE : (cc + 1) * WIDE]
    remote(wsend.at[1 - c], wrecv.at[d], w_send, w_recv.at[y], 2 * line + 1 - c, m).start()
    pltpu.make_async_copy(wsend.at[c], wrecv.at[d], w_recv.at[y]).start()
    lax.fori_loop(1, 8, w_step, 0)

    for dj in range(1, RING):
        a_arrival(dj).wait_recv()
    ro = lax.broadcasted_iota(jnp.int32, (128, 128), 0)
    co = lax.broadcasted_iota(jnp.int32, (128, 128), 1)
    want = lax.bitwise_and(lax.shift_right_logical(ro, 1), 7) * 16
    want = want + lax.shift_right_logical(ro, 4) * 2 + lax.bitwise_and(ro, 1)
    perm = (co == want).astype(F32).astype(BF16)
    regrouped = jnp.dot(perm, arecv[...].reshape(128, HIDDEN), preferred_element_type=F32)
    bsend[...] = regrouped.astype(BF16).reshape(RING, 16, HIDDEN)
    r_out = lax.rem(y + z, RING)
    r_in = mod8(j - y - z)

    def b_target(dy):
        yg = mod8(y + dy)
        return yg, yg * RING + mod8(j - y - z - yg)

    def b_copy(dy):
        yg, gl = b_target(dy)
        return remote(
            bsend.at[yg], afull.at[r_out * RING + y], b_send.at[yg], b_recv, 2 * gl + c, m
        )

    for dy in range(RING):
        yg, gl = b_target(dy)

        @pl.when(gl != line)
        def _():
            b_copy(dy).start()

        @pl.when(gl == line)
        def _():
            pltpu.make_async_copy(bsend.at[yg], afull.at[r_out * RING + y], b_recv).start()

    for dj in range(1, RING):
        js = lax.rem(j + dj, RING)
        remote(kout, kline.at[js], k_send.at[dj], k_recv.at[js], d, m).wait_recv()
    kout[...] = sum(kline[n] for n in range(RING))
    kfin[g] = kout[g]

    def l_copy(dg):
        gt = mod8(g + dg)
        return remote(kout.at[gt], kfin.at[g], l_send.at[dg], l_recv.at[g], fellow(f, gt), m)

    for dg in range(1, RING):
        l_copy(dg).start()

    lax.fori_loop(8, 14, w_step, 0)

    mine = afull.at[pl.ds(r_in * RING, RING)]
    drain(mine, b_recv)

    def gathered(js):
        return mod8(js - y - z)

    def c_copy(dx, js):
        r = gathered(js)
        part = afull.at[pl.ds(r * RING, RING)]
        dt = 2 * line + (1 - c if dx == 0 else c)
        sem = c_send.at[dx] if js is j else c_send.at[4 + lax.rem(js - m + 4, 4)]
        return remote(part, part, sem, c_recv.at[r], dt, lax.rem(m + dx, 4))

    def along_x(dx):
        return c * 4 + lax.rem(m + dx, 4)

    for dx in range(4):
        c_copy(dx, j).start()

    lax.fori_loop(14, 64, w_step, 0)

    loads[2].wait()
    loads[3].wait()
    query = q_ref[0]
    cache = kv_ref[0]
    scores = (
        lax.dot_general(query, cache, (((0,), (0,)), ((), ())), preferred_element_type=F32)
        * SCORE_SCALE
    )
    span = scores.shape[1]
    live = (m * span + lax.broadcasted_iota(jnp.int32, scores.shape, 1)) < len_ref[0]
    masked = jnp.where(live, scores, -1e30)
    peak = jnp.max(masked, axis=1, keepdims=True)
    probs = jnp.where(live, jnp.exp(masked - peak), 0.0)
    total = jnp.sum(probs, axis=1, keepdims=True)
    mixed = lax.dot_general(
        probs.astype(BF16),
        cache[:LATENT],
        (((1,), (1,)), ((), ())),
        preferred_element_type=F32,
    )
    lane = lax.broadcasted_iota(jnp.int32, (128, 128), 1)
    xacc[m] = mixed.astype(BF16)
    xstat[m] = jnp.where(lane < 64, peak, total)

    def x_copies(dx):
        mt = lax.rem(m + dx, 4)
        return (
            remote(xacc.at[m], xacc.at[m], x_send.at[0, dx], x_recv.at[0, m], d, mt),
            remote(xstat.at[m], xstat.at[m], x_send.at[1, dx], x_recv.at[1, m], d, mt),
        )

    for dx in range(1, 4):
        for copy in x_copies(dx):
            copy.start()

    for dx in range(1, 4):
        js = along_x(dx)
        c_copy(0, js).wait_recv()
        c_copy(0, js).start()

    def quantize(i, _):
        ys = mod8(y - swing(lax.rem(i + RING - 1, RING)))
        rows = wrecv.at[pl.ds(16 * ys, 16)]
        drain(rows, w_recv.at[ys])
        w = rows[...].astype(F32).reshape(128, WIDE)
        at = lax.broadcasted_iota(jnp.int32, (1, 128), 1)
        row = jnp.zeros((1, 128), F32)
        for b in range(BLOCKS):
            blk = w[:, b * 128 : (b + 1) * 128]
            top = jnp.max(jnp.max(jnp.abs(blk), axis=0, keepdims=True), axis=1, keepdims=True) + EPS
            scale = top / CODE_TOP
            coded = (blk * (CODE_TOP / top)).astype(BF16)
            down_ref[pl.ds(128 * ys, 128), b * 128 : (b + 1) * 128] = coded
            usable[pl.ds(128 * ys, 128), b * 128 : (b + 1) * 128] = (
                coded.astype(F32) * scale
            ).astype(BF16)
            row = jnp.where(at == b, scale, row)
        scl[pl.ds(ys, 1), :] = row
        return 0

    lax.fori_loop(0, 4, quantize, 0)

    for dx in range(1, 4):
        ms = lax.rem(m + dx, 4)
        remote(xacc.at[ms], xacc.at[ms], x_send.at[0, dx], x_recv.at[0, ms], d, m).wait_recv()
        remote(xstat.at[ms], xstat.at[ms], x_send.at[1, dx], x_recv.at[1, ms], d, m).wait_recv()
    peaks = [xstat[s][:, 0:1] for s in range(4)]
    highest = jnp.maximum(jnp.maximum(peaks[0], peaks[1]), jnp.maximum(peaks[2], peaks[3]))
    weight = jnp.zeros((128, 1), F32)
    blend = jnp.zeros((128, LATENT), F32)
    for s in range(4):
        factor = jnp.exp(peaks[s] - highest)
        weight = weight + xstat[s][:, 64:65] * factor
        blend = blend + xacc[s].astype(F32) * factor
    ctx_ref[...] = (blend / weight).astype(BF16)
    results[3].start()

    lax.fori_loop(4, 8, quantize, 0)
    results[0].start()
    for b in range(BLOCKS):
        scale_ref[b] = jnp.sum(
            jnp.where(iota((8, 8), 0) == iota((8, 8), 1), scl[:, b : b + 1], 0.0),
            axis=0,
            keepdims=True,
        )
    results[1].start()

    for dx in range(4):
        js = (1 - c) * 4 + lax.rem(m + dx, 4)
        c_copy(0, js).wait_recv()

    def give(part, turn):
        ft = mod8(f + swing(lax.rem(turn + 1, RING)))
        src, dst = psend.at[part * RING + turn], precv.at[part * RING + f]
        return ft, src, dst, p_recv.at[part]

    def send(part, turn):
        ft, src, dst, sem = give(part, turn)
        remote(src, dst, p_send, sem, fellow(ft, g), m).start()

    def project(turn, _):
        ft = mod8(f + swing(lax.rem(turn + 1, RING)))
        parts = []
        for dg in SIDE:
            yt, zt = at(ft, mod8(g + dg))
            parts.append(afull[mod8(yt + zt) * RING + yt])
        rows = jnp.concatenate(parts, axis=0)
        out = jnp.dot(rows, usable[...], preferred_element_type=F32).astype(BF16)
        psend[turn] = out[:64]
        psend[RING + turn] = out[64:]

        @pl.when(turn < RING - 1)
        def _():
            send(0, turn)

        return 0

    lax.fori_loop(0, RING, project, 0)
    for part in range(2):
        _, src, dst, sem = give(part, RING - 1)
        pltpu.make_async_copy(src, dst, sem).start()

    def rest(turn, _):
        send(1, turn)
        return 0

    lax.fori_loop(0, RING - 1, rest, 0)

    for dg in range(1, RING):
        gs = mod8(g + dg)
        remote(kout.at[gs], kfin.at[gs], l_send.at[dg], l_recv.at[gs], d, m).wait_recv()
    mates = high3(iota((64, 128), 0)) == low3(lax.shift_right_logical(iota((64, 128), 1), 1))
    for part in range(2):
        drain(precv.at[pl.ds(part * RING, RING)], p_recv.at[part])
        for b in range(4 * part, 4 * part + 4):
            gt = mod8(g + SIDE[b])
            share = jnp.where(mates, jnp.concatenate([kfin[gt]] * RING, axis=0), 0.0)
            high = share.astype(BF16)
            low = (share - high.astype(F32)).astype(BF16)
            at_b = 16 * (b - 4 * part)
            got = precv[pl.ds(part * RING, RING), pl.ds(at_b, 16), :].reshape(128, WIDE)
            both = jnp.dot(
                jnp.concatenate([high, low], axis=0), got, preferred_element_type=F32
            )
            qsend[b] = (both[:64] + both[64:]).astype(BF16)
            if SIDE[b]:
                remote(
                    qsend.at[b], qrecv.at[b], q_send, q_recv.at[part], fellow(f, gt), m
                ).start()
            else:
                pltpu.make_async_copy(qsend.at[b], qrecv.at[b], q_recv.at[part]).start()

    drain(qrecv.at[pl.ds(0, 4)], q_recv.at[0])
    drain(qrecv.at[pl.ds(4, 4)], q_recv.at[1])
    full = qrecv[0].astype(F32)
    for b in range(1, RING):
        full = full + qrecv[b].astype(F32)
    moesend[...] = full.reshape(RING, 8, WIDE).astype(BF16)

    def m_copy(dj):
        jt = lax.rem(j + dj, RING)
        dt, mt = mate(jt)
        return remote(moesend.at[jt], moerecv.at[j], m_send.at[dj], m_recv.at[j], dt, mt)

    for dj in range(1, RING):
        m_copy(dj).start()
    moerecv[j] = moesend[j]
    for dj in range(1, RING):
        js = lax.rem(j + dj, RING)
        remote(moesend.at[js], moerecv.at[js], m_send.at[dj], m_recv.at[js], d, m).wait_recv()
    for mm in range(4):
        for cc in range(2):
            start = (2 * mm + cc) * WIDE
            moe_ref[:, start : start + WIDE] = moerecv[cc * 4 + mm]
    results[2].start()

    for dj in range(1, RING):
        a_copy(dj).wait_send()
        k_copy(dj).wait_send()
        l_copy(dj).wait_send()
        m_copy(dj).wait_send()
    for dx in range(4):
        c_copy(dx, j).wait_send()
    for dx in range(1, 4):
        c_copy(0, along_x(dx)).wait_send()
        for copy in x_copies(dx):
            copy.wait_send()
    for dy in range(RING):
        yg, gl = b_target(dy)

        @pl.when(gl != line)
        def _():
            b_copy(dy).wait_send()

    drain(wsend.at[pl.ds(0, 127)], w_send)
    drain(psend.at[pl.ds(0, 14)], p_send)
    drain(qsend.at[pl.ds(0, 7)], q_send)
    for copy in results:
        copy.wait()


def hand_out(*refs):
    given, out, held, sem = refs[:4], refs[4:8], refs[8:12], refs[12]
    quarter = HIDDEN // 4
    pieces = [(0, pl.ds(n * quarter, quarter)) for n in range(4)] + [(1, None), (2, None), (3, None)]

    def copy(src, dst, n):
        which, rows = pieces[n]
        if rows is None:
            return pltpu.make_async_copy(src[which], dst[which], sem.at[n])
        return pltpu.make_async_copy(src[which].at[rows], dst[which].at[rows], sem.at[n])

    for n in range(7):
        copy(given, held, n).start()
    for n in range(7):
        copy(given, held, n).wait()
        copy(held, out, n).start()
    for n in range(7):
        copy(held, out, n).wait()


def per_device(
    train_down, owner, trainer_slot, expert_act, picks, route_logits, queries, kv_cache, lengths
):
    groups = jnp.arange(64, dtype=jnp.int32)
    source = jnp.sum(jnp.where(owner[None, :] == groups[:, None], trainer_slot[None, :], 0), axis=1)
    vmem = pl.BlockSpec(memory_space=pltpu.VMEM)
    smem = pl.BlockSpec(memory_space=pltpu.SMEM)
    dma = pltpu.SemaphoreType.DMA
    hbm = pl.BlockSpec(memory_space=pltpu.HBM)
    out_shape = (
        jax.ShapeDtypeStruct((HIDDEN, WIDE), BF16),
        jax.ShapeDtypeStruct((BLOCKS, 1, RING), F32),
        jax.ShapeDtypeStruct((8, 8 * WIDE), BF16),
        jax.ShapeDtypeStruct((128, LATENT), BF16),
    )
    found = pl.pallas_call(
        kernel,
        out_shape=out_shape,
        in_specs=[smem, smem] + [vmem] * 3 + [hbm] * 4,
        out_specs=(pl.BlockSpec(memory_space=pl.ANY),) * 4,
        scratch_shapes=[pltpu.VMEM(out.shape, out.dtype) for out in out_shape]
        + [
            pltpu.VMEM(train_down.shape, BF16),
            pltpu.VMEM(expert_act.shape, BF16),
            pltpu.VMEM((1, 576, 128), BF16),
            pltpu.VMEM((1, 576, 512), BF16),
            pltpu.VMEM((2, RING, 8, 128), F32),
            pltpu.VMEM((128, 8, WIDE), BF16),
            pltpu.VMEM((128, 8, WIDE), BF16),
            pltpu.VMEM((RING, 16, HIDDEN), BF16),
            pltpu.VMEM((RING, 16, HIDDEN), BF16),
            pltpu.VMEM((RING, 16, HIDDEN), BF16),
            pltpu.VMEM((64, 16, HIDDEN), BF16),
            pltpu.VMEM((HIDDEN, WIDE), BF16),
            pltpu.VMEM((16, 64, WIDE), BF16),
            pltpu.VMEM((16, 64, WIDE), BF16),
            pltpu.VMEM((RING, 64, WIDE), BF16),
            pltpu.VMEM((RING, 64, WIDE), BF16),
            pltpu.VMEM((RING, RING, 8, 128), F32),
            pltpu.VMEM((RING, 8, 128), F32),
            pltpu.VMEM((RING, 8, 128), F32),
            pltpu.VMEM((4, 128, LATENT), BF16),
            pltpu.VMEM((4, 128, 128), F32),
            pltpu.VMEM((RING, 8, WIDE), BF16),
            pltpu.VMEM((RING, 8, WIDE), BF16),
            pltpu.VMEM((RING, 128), F32),
            dma((4,)),
            dma((4,)),
            dma((RING,)),
            dma((RING,)),
            dma((RING,)),
            dma,
            dma((RING,)),
            dma((RING,)),
            dma((RING,)),
            dma((RING,)),
            dma((RING,)),
            dma((RING,)),
            dma,
            dma((RING,)),
            dma,
            dma((2,)),
            dma,
            dma((2,)),
            dma((2, 4)),
            dma((2, 4)),
            dma((RING,)),
            dma((RING,)),
        ],
        compiler_params=pltpu.CompilerParams(
            collective_id=0, has_side_effects=True, vmem_limit_bytes=LIMIT
        ),
        cost_estimate=pl.CostEstimate(
            flops=2_200_000_000, bytes_accessed=8_000_000, transcendentals=70_000
        ),
    )(
        source,
        lengths,
        owner.reshape(1, 64),
        picks,
        route_logits,
        train_down,
        expert_act,
        queries.transpose(0, 2, 1),
        kv_cache.transpose(0, 2, 1),
    )
    anywhere = pl.BlockSpec(memory_space=pl.ANY)
    down, scale, moe, context = pl.pallas_call(
        hand_out,
        out_shape=out_shape,
        in_specs=[anywhere] * 4,
        out_specs=(anywhere,) * 4,
        scratch_shapes=[pltpu.VMEM(out.shape, out.dtype) for out in out_shape] + [dma((7,))],
        compiler_params=pltpu.CompilerParams(vmem_limit_bytes=LIMIT),
    )(*found)
    return (
        down.reshape(1, HIDDEN, WIDE),
        scale.transpose(1, 2, 0),
        moe,
        context.reshape(1, 128, LATENT),
    )


def solution(mesh):
    placed = (
        P(None, "dp", "mp"),
        P(),
        P(),
        P(("dp", "mp"), None, None),
        P(("dp", "mp"), None),
        P(("dp", "mp"), None),
        P("dp", None, None),
        P("dp", "mp", None),
        P("dp"),
    )
    return jax.shard_map(
        per_device,
        mesh=mesh,
        in_specs=placed,
        out_specs=(
            P("dp", None, "mp"),
            P("dp", None, "mp"),
            P(("dp", "mp"), None),
            P("dp", None, None),
        ),
        check_vma=False,
    )
```

time: 144 us -> 121 us (0.84)
  Pallas kernels: 130 us -> 118 us
  local copies, waits for them, and re-layouts: 8.92 us -> 0 us
    pallas_call x1 -> x2, Pallas kernels: 130 us -> 118 us  [the longest x1 116 us: per_device(): pl.pallas_call(kernel, out_shape=out_shape, in_specs=[smem, smem] + [vmem...]
    unnamed x10 -> x0, local copies, waits for them, and re-layouts: 8 us -> none
where the time goes in v2:
time: 121 us
  Pallas kernels  118 us (98%)
  other arithmetic  1.3 us (1%)
  between operations  1.29 us (1%)
    pallas_call x1, Pallas kernels, per_device(): pl.pallas_call(kernel, out_shape=out_shape, in_specs=[smem, smem] + [vmem...  116 us

profile of v2, /device:TPU:1, one launch (start us, length us, event | category | flops | bytes accessed | tf_op | source)
XLA Modules:
  0.0 120.7 jit_solution(13185214412199398982)
XLA Ops:
  1.3 1.3 %select_reduce_fusion.src_ref = s32[64]{0:T(128)} fusion(s32[64]{0:T(128)} %param.11, s32[64]{0:T(128)} %param.10), kind=kLoop, calls=%fused_computation | loop fusion | flops 12224 | bytes 768 | tf_op jit(solution)/shard_map/reduce_sum | solution.py:558
  2.6 115.7 %shard_map.120 = (bf16[1024,896]{1,0:T(8,128)(2,1)}, f32[7,1,8]{2,1,0:T(1,128)}, bf16[8,7168]{1,0:T(8,128)(2,1)}, bf16[128,512]{1,0:T(8,128)(2,1)}) custom-call(s32[64]{0:T(128)} %select_reduce_fusion.src_ref, s32[1]{0:T(128)S(6)} %copy.13.len_ref, s32[1,64]{1,0:T(1,128)} %bitcast.11, s32[8,8]{1,0:T(8,128)} %picks_ref.1, f32[8,8]{1,0:T(8,128)} %logit_ref.1, ...), custom_call_target="tpu_custom_call" | custom-call | flops 2200000000 | bytes 8000000 | tf_op jit(solution)/shard_map/pallas_call | solution.py:569
  118.3 2.4 %shard_map.121 = (bf16[1024,896]{1,0:T(8,128)(2,1)}, f32[7,1,8]{2,1,0:T(1,128)}, bf16[8,7168]{1,0:T(8,128)(2,1)}, bf16[128,512]{1,0:T(8,128)(2,1)}) custom-call(bf16[1024,896]{1,0:T(8,128)(2,1)} %get-tuple-element.12.refs_0_, f32[7,1,8]{2,1,0:T(1,128)} %get-tuple-element.13.refs_1_, bf16[8,7168]{1,0:T(8,128)(2,1)} %get-tuple-element.14.refs_2_, ...), custom_call_target="tpu_custom_call" | custom-call | tf_op jit(solution)/shard_map/pallas_call | solution.py:641

commit v3 on v2

--- a/solution.py
+++ b/solution.py
@@ -20,6 +20,7 @@
 BLOCKS = WIDE // 128
 LIMIT = 64 * 1024 * 1024
 SIDE = (1, 7, 3, 5, 2, 6, 4, 0)
+PARTS = ((0, 4), (4, 7))
 
 
 def mod8(v):
@@ -239,27 +240,49 @@
     for dj in range(1, RING):
         k_copy(dj).start()
 
+    def columns(part):
+        first, last = PARTS[part]
+        return slice(first * 128, last * 128)
+
     def w_line(t):
         dy, dz = offset(lax.div(t, RING), lax.rem(t, RING))
         return mod8(y + dy) * RING + mod8(z + dz)
 
+    def w_give(t, cc, part):
+        cols = columns(part)
+        return wsend.at[2 * t + cc, :, cols], wrecv.at[d, :, cols], w_recv.at[part, y]
+
+    def w_send_line(t, part):
+        lt = w_line(t)
+        for cc in range(2):
+            src, dst, sem = w_give(t, cc, part)
+            remote(src, dst, w_send, sem, 2 * lt + cc, m).start()
+
     def w_step(t, _):
-        lt = w_line(t)
-        blk = td_ref[src_ref[lt]]
+        blk = td_ref[src_ref[w_line(t)]]
         for cc in range(2):
             wsend[2 * t + cc] = blk[:, cc * WIDE : (cc + 1) * WIDE]
-        for cc in range(2):
-            dt = 2 * lt + cc
-            remote(wsend.at[2 * t + cc], wrecv.at[d], w_send, w_recv.at[y], dt, m).start()
+        w_send_line(t, 0)
         return 0
+
+    def w_rest(t, _):
+        w_send_line(t, 1)
+        return 0
+
+    def w_own(part):
+        src, dst, sem = w_give(0, 1 - c, part)
+        remote(src, dst, w_send, sem, 2 * line + 1 - c, m).start()
+        src, dst, sem = w_give(0, c, part)
+        pltpu.make_async_copy(src, dst, sem).start()
 
     loads[1].wait()
     own = td_ref[src_ref[line]]
     for cc in range(2):
         wsend[cc] = own[:, cc * WIDE : (cc + 1) * WIDE]
-    remote(wsend.at[1 - c], wrecv.at[d], w_send, w_recv.at[y], 2 * line + 1 - c, m).start()
-    pltpu.make_async_copy(wsend.at[c], wrecv.at[d], w_recv.at[y]).start()
-    lax.fori_loop(1, 8, w_step, 0)
+    w_own(0)
+    lax.fori_loop(1, 12, w_step, 0)
+
+    lax.fori_loop(12, 24, w_step, 0)
 
     for dj in range(1, RING):
         a_arrival(dj).wait_recv()
@@ -307,7 +330,7 @@
     for dg in range(1, RING):
         l_copy(dg).start()
 
-    lax.fori_loop(8, 14, w_step, 0)
+    lax.fori_loop(24, 48, w_step, 0)
 
     mine = afull.at[pl.ds(r_in * RING, RING)]
     drain(mine, b_recv)
@@ -328,7 +351,16 @@
     for dx in range(4):
         c_copy(dx, j).start()
 
-    lax.fori_loop(14, 64, w_step, 0)
+    lax.fori_loop(48, 64, w_step, 0)
+    w_own(1)
+    lax.fori_loop(1, 32, w_rest, 0)
+
+    for dx in range(1, 4):
+        js = along_x(dx)
+        c_copy(0, js).wait_recv()
+        c_copy(0, js).start()
+
+    lax.fori_loop(32, 64, w_rest, 0)
 
     loads[2].wait()
     loads[3].wait()
@@ -365,20 +397,15 @@
         for copy in x_copies(dx):
             copy.start()
 
-    for dx in range(1, 4):
-        js = along_x(dx)
-        c_copy(0, js).wait_recv()
-        c_copy(0, js).start()
-
-    def quantize(i, _):
+    def quantize(part, i):
         ys = mod8(y - swing(lax.rem(i + RING - 1, RING)))
-        rows = wrecv.at[pl.ds(16 * ys, 16)]
-        drain(rows, w_recv.at[ys])
-        w = rows[...].astype(F32).reshape(128, WIDE)
-        at = lax.broadcasted_iota(jnp.int32, (1, 128), 1)
+        rows = wrecv.at[pl.ds(16 * ys, 16), :, columns(part)]
+        drain(rows, w_recv.at[part, ys])
+        first, last = PARTS[part]
+        w = rows[...].astype(F32).reshape(128, (last - first) * 128)
         row = jnp.zeros((1, 128), F32)
-        for b in range(BLOCKS):
-            blk = w[:, b * 128 : (b + 1) * 128]
+        for b in range(first, last):
+            blk = w[:, (b - first) * 128 : (b - first + 1) * 128]
             top = jnp.max(jnp.max(jnp.abs(blk), axis=0, keepdims=True), axis=1, keepdims=True) + EPS
             scale = top / CODE_TOP
             coded = (blk * (CODE_TOP / top)).astype(BF16)
@@ -386,11 +413,62 @@
             usable[pl.ds(128 * ys, 128), b * 128 : (b + 1) * 128] = (
                 coded.astype(F32) * scale
             ).astype(BF16)
-            row = jnp.where(at == b, scale, row)
-        scl[pl.ds(ys, 1), :] = row
-        return 0
-
-    lax.fori_loop(0, 4, quantize, 0)
+            row = jnp.where(iota((1, 128), 1) == b, scale, row)
+        scl[part, pl.ds(ys, 1), :] = row
+
+    def requantize(part):
+        def step(i, _):
+            quantize(part, i)
+            return 0
+
+        lax.fori_loop(0, RING, step, 0)
+
+    requantize(0)
+
+    for dx in range(4):
+        js = (1 - c) * 4 + lax.rem(m + dx, 4)
+        c_copy(0, js).wait_recv()
+
+    def give(part, turn):
+        ft = mod8(f + swing(lax.rem(turn + 1, RING)))
+        cols = columns(part)
+        return ft, psend.at[turn, :, cols], precv.at[f, :, cols], p_recv.at[part]
+
+    def project(part):
+        def step(turn, _):
+            ft, src, dst, sem = give(part, turn)
+            parts = []
+            for dg in SIDE:
+                yt, zt = at(ft, mod8(g + dg))
+                parts.append(afull[mod8(yt + zt) * RING + yt])
+            rows = jnp.concatenate(parts, axis=0)
+            weights = usable[:, columns(part)]
+            src[...] = jnp.dot(rows, weights, preferred_element_type=F32).astype(BF16)
+
+            @pl.when(turn < RING - 1)
+            def _():
+                remote(src, dst, p_send, sem, fellow(ft, g), m).start()
+
+            @pl.when(turn == RING - 1)
+            def _():
+                pltpu.make_async_copy(src, dst, sem).start()
+
+            return 0
+
+        lax.fori_loop(0, RING, step, 0)
+
+    project(0)
+    requantize(1)
+    results[0].start()
+    for b in range(BLOCKS):
+        scale_ref[b] = jnp.sum(
+            jnp.where(iota((8, 8), 0) == iota((8, 8), 1), scl[b // 4, :, b : b + 1], 0.0),
+            axis=0,
+            keepdims=True,
+        )
+    results[1].start()
+
+    project(1)
 
     for dx in range(1, 4):
         ms = lax.rem(m + dx, 4)
@@ -407,87 +485,34 @@
     ctx_ref[...] = (blend / weight).astype(BF16)
     results[3].start()
 
-    lax.fori_loop(4, 8, quantize, 0)
-    results[0].start()
-    for b in range(BLOCKS):
-        scale_ref[b] = jnp.sum(
-            jnp.where(iota((8, 8), 0) == iota((8, 8), 1), scl[:, b : b + 1], 0.0),
-            axis=0,
-            keepdims=True,
-        )
-    results[1].start()
-
-    for dx in range(4):
-        js = (1 - c) * 4 + lax.rem(m + dx, 4)
-        c_copy(0, js).wait_recv()
-
-    def give(part, turn):
-        ft = mod8(f + swing(lax.rem(turn + 1, RING)))
-        src, dst = psend.at[part * RING + turn], precv.at[part * RING + f]
-        return ft, src, dst, p_recv.at[part]
-
-    def send(part, turn):
-        ft, src, dst, sem = give(part, turn)
-        remote(src, dst, p_send, sem, fellow(ft, g), m).start()
-
-    def project(turn, _):
-        ft = mod8(f + swing(lax.rem(turn + 1, RING)))
-        parts = []
-        for dg in SIDE:
-            yt, zt = at(ft, mod8(g + dg))
-            parts.append(afull[mod8(yt + zt) * RING + yt])
-        rows = jnp.concatenate(parts, axis=0)
-        out = jnp.dot(rows, usable[...], preferred_element_type=F32).astype(BF16)
-        psend[turn] = out[:64]
-        psend[RING + turn] = out[64:]
-
-        @pl.when(turn < RING - 1)
-        def _():
-            send(0, turn)
-
-        return 0
-
-    lax.fori_loop(0, RING, project, 0)
-    for part in range(2):
-        _, src, dst, sem = give(part, RING - 1)
-        pltpu.make_async_copy(src, dst, sem).start()
-
-    def rest(turn, _):
-        send(1, turn)
-        return 0
-
-    lax.fori_loop(0, RING - 1, rest, 0)
-
     for dg in range(1, RING):
         gs = mod8(g + dg)
         remote(kout.at[gs], kfin.at[gs], l_send.at[dg], l_recv.at[gs], d, m).wait_recv()
     mates = high3(iota((64, 128), 0)) == low3(lax.shift_right_logical(iota((64, 128), 1), 1))
     for part in range(2):
-        drain(precv.at[pl.ds(part * RING, RING)], p_recv.at[part])
-        for b in range(4 * part, 4 * part + 4):
+        cols = columns(part)
+        drain(precv.at[:, :, cols], p_recv.at[part])
+        for b in range(RING):
             gt = mod8(g + SIDE[b])
             share = jnp.where(mates, jnp.concatenate([kfin[gt]] * RING, axis=0), 0.0)
             high = share.astype(BF16)
             low = (share - high.astype(F32)).astype(BF16)
-            at_b = 16 * (b - 4 * part)
-            got = precv[pl.ds(part * RING, RING), pl.ds(at_b, 16), :].reshape(128, WIDE)
-            both = jnp.dot(
-                jnp.concatenate([high, low], axis=0), got, preferred_element_type=F32
-            )
-            qsend[b] = (both[:64] + both[64:]).astype(BF16)
+            got = precv[:, 16 * b : 16 * b + 16, cols].reshape(128, cols.stop - cols.start)
+            both = jnp.dot(jnp.concatenate([high, low], axis=0), got, preferred_element_type=F32)
+            src, dst = qsend.at[b, :, cols], qrecv.at[b, :, cols]
+            src[...] = (both[:64] + both[64:]).astype(BF16)
             if SIDE[b]:
-                remote(
-                    qsend.at[b], qrecv.at[b], q_send, q_recv.at[part], fellow(f, gt), m
-                ).start()
+                remote(src, dst, q_send, q_recv.at[part], fellow(f, gt), m).start()
             else:
-                pltpu.make_async_copy(qsend.at[b], qrecv.at[b], q_recv.at[part]).start()
-
-    drain(qrecv.at[pl.ds(0, 4)], q_recv.at[0])
-    drain(qrecv.at[pl.ds(4, 4)], q_recv.at[1])
-    full = qrecv[0].astype(F32)
-    for b in range(1, RING):
-        full = full + qrecv[b].astype(F32)
-    moesend[...] = full.reshape(RING, 8, WIDE).astype(BF16)
+                pltpu.make_async_copy(src, dst, q_recv.at[part]).start()
+
+    for part in range(2):
+        cols = columns(part)
+        drain(qrecv.at[:, :, cols], q_recv.at[part])
+        full = qrecv[0, :, cols].astype(F32)
+        for b in range(1, RING):
+            full = full + qrecv[b, :, cols].astype(F32)
+        moesend[:, :, cols] = full.reshape(RING, 8, cols.stop - cols.start).astype(BF16)
 
     def m_copy(dj):
         jt = lax.rem(j + dj, RING)
@@ -525,7 +550,7 @@
             b_copy(dy).wait_send()
 
     drain(wsend.at[pl.ds(0, 127)], w_send)
-    drain(psend.at[pl.ds(0, 14)], p_send)
+    drain(psend.at[pl.ds(0, 7)], p_send)
     drain(qsend.at[pl.ds(0, 7)], q_send)
     for copy in results:
         copy.wait()
@@ -585,8 +610,8 @@
             pltpu.VMEM((RING, 16, HIDDEN), BF16),
             pltpu.VMEM((64, 16, HIDDEN), BF16),
             pltpu.VMEM((HIDDEN, WIDE), BF16),
-            pltpu.VMEM((16, 64, WIDE), BF16),
-            pltpu.VMEM((16, 64, WIDE), BF16),
+            pltpu.VMEM((RING, 128, WIDE), BF16),
+            pltpu.VMEM((RING, 128, WIDE), BF16),
             pltpu.VMEM((RING, 64, WIDE), BF16),
             pltpu.VMEM((RING, 64, WIDE), BF16),
             pltpu.VMEM((RING, RING, 8, 128), F32),
@@ -596,7 +621,7 @@
             pltpu.VMEM((4, 128, 128), F32),
             pltpu.VMEM((RING, 8, WIDE), BF16),
             pltpu.VMEM((RING, 8, WIDE), BF16),
-            pltpu.VMEM((RING, 128), F32),
+            pltpu.VMEM((2, RING, 128), F32),
             dma((4,)),
             dma((4,)),
             dma((RING,)),
@@ -610,7 +635,7 @@
             dma((RING,)),
             dma((RING,)),
             dma,
-            dma((RING,)),
+            dma((2, RING)),
             dma,
             dma((2,)),
             dma,

time: 121 us -> 112 us (0.926)
  Pallas kernels: 118 us -> 109 us
    pallas_call x1, Pallas kernels: 116 us -> 107 us  [per_device(): pl.pallas_call(kernel, out_shape=out_shape, in_specs=[smem, smem] + [vmem...]
where the time goes in v3:
time: 112 us
  Pallas kernels  109 us (97%)
  other arithmetic  1.3 us (1%)
  between operations  1.29 us (1%)
    pallas_call x1, Pallas kernels, per_device(): pl.pallas_call(kernel, out_shape=out_shape, in_specs=[smem, smem] + [vmem...  107 us
    pallas_call x1, Pallas kernels, per_device(): pl.pallas_call(hand_out, out_shape=out_shape, in_specs=[anywhere] * 4, ou...  2.38 us

profile of v3, /device:TPU:1, one launch (start us, length us, event | category | flops | bytes accessed | tf_op | source)
XLA Modules:
  0.0 111.6 jit_solution(10696152635877726237)
XLA Ops:
  1.3 1.3 %select_reduce_fusion.src_ref = s32[64]{0:T(128)} fusion(s32[64]{0:T(128)} %param.11, s32[64]{0:T(128)} %param.10), kind=kLoop, calls=%fused_computation | loop fusion | flops 12224 | bytes 768 | tf_op jit(solution)/shard_map/reduce_sum | solution.py:583
  2.6 106.6 %shard_map.120 = (bf16[1024,896]{1,0:T(8,128)(2,1)}, f32[7,1,8]{2,1,0:T(1,128)}, bf16[8,7168]{1,0:T(8,128)(2,1)}, bf16[128,512]{1,0:T(8,128)(2,1)}) custom-call(s32[64]{0:T(128)} %select_reduce_fusion.src_ref, s32[1]{0:T(128)S(6)} %copy.13.len_ref, s32[1,64]{1,0:T(1,128)} %bitcast.11, s32[8,8]{1,0:T(8,128)} %picks_ref.1, f32[8,8]{1,0:T(8,128)} %logit_ref.1, ...), custom_call_target="tpu_custom_call" | custom-call | flops 2200000000 | bytes 8000000 | tf_op jit(solution)/shard_map/pallas_call | solution.py:594
  109.2 2.4 %shard_map.121 = (bf16[1024,896]{1,0:T(8,128)(2,1)}, f32[7,1,8]{2,1,0:T(1,128)}, bf16[8,7168]{1,0:T(8,128)(2,1)}, bf16[128,512]{1,0:T(8,128)(2,1)}) custom-call(bf16[1024,896]{1,0:T(8,128)(2,1)} %get-tuple-element.12.refs_0_, f32[7,1,8]{2,1,0:T(1,128)} %get-tuple-element.13.refs_1_, bf16[8,7168]{1,0:T(8,128)(2,1)} %get-tuple-element.14.refs_2_, ...), custom_call_target="tpu_custom_call" | custom-call | tf_op jit(solution)/shard_map/pallas_call | solution.py:666

commit v4 on v3

--- a/solution.py
+++ b/solution.py
@@ -20,7 +20,7 @@
 BLOCKS = WIDE // 128
 LIMIT = 64 * 1024 * 1024
 SIDE = (1, 7, 3, 5, 2, 6, 4, 0)
-PARTS = ((0, 4), (4, 7))
+PARTS = ((0, 5), (5, 7))
 
 
 def mod8(v):
@@ -280,9 +280,9 @@
     for cc in range(2):
         wsend[cc] = own[:, cc * WIDE : (cc + 1) * WIDE]
     w_own(0)
-    lax.fori_loop(1, 12, w_step, 0)
-
-    lax.fori_loop(12, 24, w_step, 0)
+    lax.fori_loop(1, 18, w_step, 0)
+
+    lax.fori_loop(18, 32, w_step, 0)
 
     for dj in range(1, RING):
         a_arrival(dj).wait_recv()
@@ -330,7 +330,7 @@
     for dg in range(1, RING):
         l_copy(dg).start()
 
-    lax.fori_loop(24, 48, w_step, 0)
+    lax.fori_loop(32, 60, w_step, 0)
 
     mine = afull.at[pl.ds(r_in * RING, RING)]
     drain(mine, b_recv)
@@ -351,16 +351,16 @@
     for dx in range(4):
         c_copy(dx, j).start()
 
-    lax.fori_loop(48, 64, w_step, 0)
+    lax.fori_loop(60, 64, w_step, 0)
     w_own(1)
-    lax.fori_loop(1, 32, w_rest, 0)
+    lax.fori_loop(1, 48, w_rest, 0)
 
     for dx in range(1, 4):
         js = along_x(dx)
         c_copy(0, js).wait_recv()
         c_copy(0, js).start()
 
-    lax.fori_loop(32, 64, w_rest, 0)
+    lax.fori_loop(48, 64, w_rest, 0)
 
     loads[2].wait()
     loads[3].wait()
@@ -462,7 +462,7 @@
     results[0].start()
     for b in range(BLOCKS):
         scale_ref[b] = jnp.sum(
-            jnp.where(iota((8, 8), 0) == iota((8, 8), 1), scl[b // 4, :, b : b + 1], 0.0),
+            jnp.where(iota((8, 8), 0) == iota((8, 8), 1), scl[b // 5, :, b : b + 1], 0.0),
             axis=0,
             keepdims=True,
         )

time: 112 us -> 109 us (0.973)
  Pallas kernels: 109 us -> 106 us
    pallas_call x1, Pallas kernels: 107 us -> 103 us  [per_device(): pl.pallas_call(kernel, out_shape=out_shape, in_specs=[smem, smem] + [vmem...]
where the time goes in v4:
time: 109 us; the launch traced here: 108 us
  Pallas kernels  106 us (97%)
  other arithmetic  1.3 us (1%)
  between operations  1.29 us (1%)
    pallas_call x1, Pallas kernels, per_device(): pl.pallas_call(kernel, out_shape=out_shape, in_specs=[smem, smem] + [vmem...  103 us
    pallas_call x1, Pallas kernels, per_device(): pl.pallas_call(hand_out, out_shape=out_shape, in_specs=[anywhere] * 4, ou...  2.38 us

profile of v4, /device:TPU:1, one launch (start us, length us, event | category | flops | bytes accessed | tf_op | source)
XLA Modules:
  0.0 108.4 jit_solution(7394353357942040694)
XLA Ops:
  1.3 1.3 %select_reduce_fusion.src_ref = s32[64]{0:T(128)} fusion(s32[64]{0:T(128)} %param.11, s32[64]{0:T(128)} %param.10), kind=kLoop, calls=%fused_computation | loop fusion | flops 12224 | bytes 768 | tf_op jit(solution)/shard_map/reduce_sum | solution.py:583
  2.6 103.5 %shard_map.120 = (bf16[1024,896]{1,0:T(8,128)(2,1)}, f32[7,1,8]{2,1,0:T(1,128)}, bf16[8,7168]{1,0:T(8,128)(2,1)}, bf16[128,512]{1,0:T(8,128)(2,1)}) custom-call(s32[64]{0:T(128)} %select_reduce_fusion.src_ref, s32[1]{0:T(128)S(6)} %copy.13.len_ref, s32[1,64]{1,0:T(1,128)} %bitcast.11, s32[8,8]{1,0:T(8,128)} %picks_ref.1, f32[8,8]{1,0:T(8,128)} %logit_ref.1, ...), custom_call_target="tpu_custom_call" | custom-call | flops 2200000000 | bytes 8000000 | tf_op jit(solution)/shard_map/pallas_call | solution.py:594
  106.0 2.4 %shard_map.121 = (bf16[1024,896]{1,0:T(8,128)(2,1)}, f32[7,1,8]{2,1,0:T(1,128)}, bf16[8,7168]{1,0:T(8,128)(2,1)}, bf16[128,512]{1,0:T(8,128)(2,1)}) custom-call(bf16[1024,896]{1,0:T(8,128)(2,1)} %get-tuple-element.12.refs_0_, f32[7,1,8]{2,1,0:T(1,128)} %get-tuple-element.13.refs_1_, bf16[8,7168]{1,0:T(8,128)(2,1)} %get-tuple-element.14.refs_2_, ...), custom_call_target="tpu_custom_call" | custom-call | tf_op jit(solution)/shard_map/pallas_call | solution.py:666
